TPU v7x, 32 devices: a whole 2x2x4 slice. The times are simulated.
32 devices in a mesh: groups: 2 (over x), batch: 8 (over z, y), tensor: 2 (over core).
Axes of the slice: x: 2, y: 2, z: 4, core: 2. Of those that a mesh axis runs over, the one named last changes fastest.
Arguments:
- teacher_rows: bfloat16 [8192, 6144], P(('groups', 'batch'), 'tensor'), parts along dimension 0, may hold values from -6 to 6
- teacher_gain: bfloat16 [6144], P('tensor'), may hold values from 0.099609375 to 1.8984375
- head_weight: bfloat16 [6144, 1024], P('tensor'), may hold values from -0.078125 to 0.078125
- student_slot: int32 [8192], P(('groups', 'batch')), parts along dimension 0, may hold values from 0 to 4095, as said below
- student_rows: bfloat16 [8192, 1024], P(('groups', 'batch')), parts along dimension 0, may hold values from -6 to 6
- student_gain: bfloat16 [1024], replicated, may hold values from 0.099609375 to 1.8984375
- up_weight: bfloat16 [1024, 2048], P(None, 'tensor'), may hold values from -0.1875 to 0.1875
- down_weight: bfloat16 [2048, 1024], P('tensor'), may hold values from -0.125 to 0.125
Outputs:
- grad_up: float32 [2048, 2048], P(('groups', 'batch'), 'tensor'), parts along dimension 0
- grad_down: float32 [4096, 1024], P(('groups', 'tensor'), 'batch'), parts along dimension 0
There are 2 independent parts, one for each index of `groups`. A program takes and returns all parts, laid end to end along the dimension named above; an argument that names none is the same for every part. Nothing has to cross between parts.
Inputs may be any that keep to these rules, and one draw needn't show every extreme that they name: `student_slot`: A permutation of the 4096 rows. The rows of one index of batch send at most 128 rows into any one block of 512 rows of the student order, and exactly 128 into some.
All inputs are finite; a program needn't handle non-finite values.
Results may differ from a plain program's by a relative error of at most 0.0044.
Values may be sent and summed in bfloat16 or wider, within the bound.
A program may use at most 128 MiB of HBM per device.

v0:
```python
import jax
import jax.numpy as jnp
from jax import lax
from jax.sharding import PartitionSpec as P

EPS = 1e-06


def gelu_tanh(value):
    return jax.nn.gelu(value, approximate=True)


def scale_rows(values, mean, var, gain):
    scaled = (
        (values - mean[:, None]) * lax.rsqrt(var + EPS)[:, None] * gain.astype(jnp.float32)[None, :]
    )
    return scaled.astype(jnp.bfloat16)


def move_rows(values, slots):
    peers = lax.axis_size("batch")
    rows = slots.shape[0]
    capacity = 2 * rows // peers
    owner = slots // rows
    local = slots % rows
    onehot = (owner[:, None] == jnp.arange(peers, dtype=jnp.int32)[None, :]).astype(jnp.int32)
    rank = jnp.sum((jnp.cumsum(onehot, axis=0) - onehot) * onehot, axis=1)
    flat = owner * capacity + rank
    buffer = jnp.zeros((peers * capacity, values.shape[1]), values.dtype).at[flat].set(values)
    places = jnp.full((peers * capacity,), rows, jnp.int32).at[flat].set(local)
    got, where = (
        lax.all_to_all(
            buffer.reshape(peers, capacity, values.shape[1]),
            "batch",
            split_axis=0,
            concat_axis=0,
            tiled=True,
        ),
        lax.all_to_all(
            places.reshape(peers, capacity), "batch", split_axis=0, concat_axis=0, tiled=True
        ),
    )
    return (
        jnp.zeros_like(values)
        .at[where.reshape(-1)]
        .set(got.reshape(peers * capacity, values.shape[1]), mode="drop")
    )


def body(
    teacher_rows,
    teacher_gain,
    head_weight,
    student_slot,
    student_rows,
    student_gain,
    up_weight,
    down_weight,
):
    peers = lax.axis_size("batch")
    rows = teacher_rows.shape[0]
    teacher_vals = teacher_rows.astype(jnp.float32)
    width_t = teacher_rows.shape[1] * lax.axis_size("tensor")
    total, total_sq = lax.psum(
        (jnp.sum(teacher_vals, axis=1), jnp.sum(teacher_vals * teacher_vals, axis=1)), "tensor"
    )
    mean_t = total / width_t
    var_t = total_sq / width_t - mean_t * mean_t
    normed_t = scale_rows(teacher_vals, mean_t, var_t, teacher_gain)
    partial_value = jnp.dot(normed_t, head_weight, preferred_element_type=jnp.float32)
    target = lax.psum(partial_value, "tensor").astype(jnp.bfloat16)
    arrived = move_rows(target, student_slot)
    student_vals = student_rows.astype(jnp.float32)
    width_s = student_rows.shape[1]
    mean_s = jnp.sum(student_vals, axis=1) / width_s
    var_s = jnp.sum(student_vals * student_vals, axis=1) / width_s - mean_s * mean_s
    normed_s = scale_rows(student_vals, mean_s, var_s, student_gain)
    pre = jnp.dot(normed_s, up_weight, preferred_element_type=jnp.float32)
    act_value, pull = jax.vjp(gelu_tanh, pre)
    act = act_value.astype(jnp.bfloat16)
    out_part = jnp.dot(act, down_weight, preferred_element_type=jnp.float32)
    scale = lax.rsqrt(jnp.asarray(rows * peers, jnp.float32))
    out_full = lax.psum(out_part, "tensor")
    diff = ((out_full - arrived.astype(jnp.float32)) * scale).astype(jnp.bfloat16)
    back = jnp.einsum("td,hd->th", diff, down_weight, preferred_element_type=jnp.float32)
    dpre = pull(back)[0].astype(jnp.bfloat16)
    local_up = jnp.einsum("ti,th->ih", normed_s, dpre, preferred_element_type=jnp.float32)
    local_down = jnp.einsum("th,td->hd", act, diff, preferred_element_type=jnp.float32)
    grad_up, grad_down = (
        lax.psum_scatter(local_up, "batch", scatter_dimension=0, tiled=True),
        lax.psum_scatter(local_down, "batch", scatter_dimension=1, tiled=True),
    )
    return (grad_up, grad_down)


def solution(mesh):
    return jax.shard_map(
        body,
        mesh=mesh,
        in_specs=(
            P(("groups", "batch"), "tensor"),
            P("tensor"),
            P("tensor", None),
            P(("groups", "batch")),
            P(("groups", "batch"), None),
            P(),
            P(None, "tensor"),
            P("tensor", None),
        ),
        out_specs=(P(("groups", "batch"), "tensor"), P(("groups", "tensor"), "batch")),
        check_vma=False,
    )
```

profile of v0, /device:TPU:0, one launch (start us, length us, event | category | flops | bytes accessed | tf_op | source)
XLA Modules:
  0.0 314.6 jit_solution(8172282805101675712)
XLA Ops:
  7.2 0.0 copy-start
  7.2 0.0 all-reduce.4.cloned.1.call-start
  7.3 3.0 convert_reduce_fusion
  10.3 0.4 convert_reduce_fusion.1
  10.8 2.6 all-reduce
  13.4 0.0 copy-start.6
  13.4 3.0 fusion.42
  16.4 0.0 copy-start.1
  16.5 2.7 fusion.44
  19.2 0.4 copy-done.1
  19.6 4.8 %fusion.4 = f32[512,1024]{1,0:T(8,128)} fusion(bf16[3072,1024]{1,0:T(8,128)(2,1)S(1)} %copy-done.6, bf16[512,3072]{1,0:T(8,128)(2,1)S(1)} %copy-done.1, f32[3072]{0:T(1024)S(1)} %convert_element_type.47, f32[512]{0:T(512)S(1)} %get-tuple-element.13, f32[512]{0:T(512)S(1)} %get-tuple-element.12), kind=kOutput, calls=%fused_computation.10 | convolution fusion | flops 3229089792 | bytes 11550720 | tf_op jit(solution)/shard_map/dot_general | solution.py:70
  24.4 0.0 all-reduce.4.cloned.1.call-update
  24.4 0.7 copy-done.5
  25.1 1.1 reduce-window.6
  26.3 0.2 slice_reduce_fusion
  26.5 0.1 fusion.28
  26.6 3.0 scatter_custom_fusion
  29.6 7.2 %all-to-all-start = ((s32[8,1,128]{2,1,0:T(1,128)}), s32[8,1,128]{2,1,0:T(1,128)S(1)}, u32[]{:S(2)}, u32[]{:S(2)}) async-start(s32[8,1,128]{2,1,0:T(1,128)} %bitcast.3), calls=%async_computation | async-start | bytes 8192 | tf_op jit(solution)/shard_map/all_to_all | solution.py:39
  36.8 18.9 %all-reduce.4.cloned.1.call-done = (f32[512,1024]{1,0:T(8,128)}, f32[512,1024]{1,0:T(8,128)}) async-done(((f32[512,1024]{1,0:T(8,128)}, f32[512,1024]{1,0:T(8,128)}), (f32[512,1024]{1,0:T(8,128)}, f32[512,1024]{1,0:T(8,128)})) %all-reduce.4.cloned.1.call-update) | async-done | bytes 4194320 | tf_op jit(solution)/shard_map/psum | solution.py:83
  55.7 5.1 %scatter_custom_fusion.1 = bf16[1024,1024]{1,0:T(8,128)(2,1)} fusion(s32[512]{0:T(512)S(1)} %compare_select_fusion.1, f32[512,1024]{1,0:T(8,128)} %get-tuple-element.9, bf16[]{:T(256)} %constant.56.clone.1), kind=kCustom, calls=%fused_computation.32 | custom fusion | flops 524288 | bytes 4194306 | tf_op jit(solution)/shard_map/scatter | solution.py:29
  60.8 0.0 all-to-all-done
  60.8 5.8 %all-to-all-start.1 = ((bf16[8,128,1024]{2,1,0:T(8,128)(2,1)}), bf16[8,128,1024]{2,1,0:T(8,128)(2,1)}, u32[]{:S(2)}, u32[]{:S(2)}) async-start(bf16[8,128,1024]{2,1,0:T(8,128)(2,1)} %bitcast.19), calls=%async_computation.1 | async-start | bytes 4194304 | tf_op jit(solution)/shard_map/all_to_all | solution.py:32
  66.6 0.2 reduce-scatter.5.cloned.1.call-start
  66.9 48.6 %all-to-all-done.1 = bf16[8,128,1024]{2,1,0:T(8,128)(2,1)} async-done(((bf16[8,128,1024]{2,1,0:T(8,128)(2,1)}), bf16[8,128,1024]{2,1,0:T(8,128)(2,1)}, u32[]{:S(2)}, u32[]{:S(2)}) %all-to-all-start.1) | async-done | bytes 2097184 | tf_op jit(solution)/shard_map/all_to_all | solution.py:32
  115.4 7.0 %scatter_custom_fusion.2 = bf16[512,1024]{1,0:T(8,128)(2,1)} fusion(s32[1024]{0:T(1024)S(1)} %bitcast.21, bf16[1024,1024]{1,0:T(8,128)(2,1)} %bitcast.7, bf16[]{:T(256)} %constant.56.clone.1), kind=kCustom, calls=%fused_computation.36 | custom fusion | bytes 1049088 | tf_op jit(solution)/shard_map/scatter | solution.py:46
  122.4 6.1 %fusion.39 = f32[1024,1024]{1,0:T(8,128)} fusion(f32[512,1024]{1,0:T(8,128)} %get-tuple-element.8, bf16[512,1024]{1,0:T(8,128)(2,1)} %scatter_custom_fusion.2, f32[512,1024]{1,0:T(8,128)} %copy-done.7), kind=kOutput, calls=%fused_computation.67 | convolution fusion | flops 1080557568 | bytes 9437184 | tf_op jit(solution)/shard_map/th,td->hd/dot_general | solution.py:88
  128.5 0.0 reduce-scatter.5.cloned.1.call-update
  128.5 0.0 reduce-scatter.3.cloned.1.call-start
  128.6 7.8 %fusion.23 = f32[1024,1024]{1,0:T(8,128)} fusion(f32[512,1024]{1,0:T(8,128)} %copy-done.7, bf16[1024,1024]{1,0:T(8,128)(2,1)S(1)} %copy-done, f32[512,1024]{1,0:T(8,128)} %get-tuple-element.8, bf16[512,1024]{1,0:T(8,128)(2,1)} %scatter_custom_fusion.2, bf16[512,1024]{1,0:T(8,128)(2,1)S(1)} %copy-done.2, f32[1024]{0:T(1024)S(1)} %convert_element_type.41, ...), kind=kOutput, calls=%fused_computation.35 | convolution fusion | flops 2162688000 | bytes 12591104 | tf_op jit(solution)/shard_map/ti,th->ih/dot_general | solution.py:87
  136.4 0.0 reduce-scatter.3.cloned.1.call-update
  136.4 79.8 %reduce-scatter.5.cloned.1.call-done = f32[1024,128]{1,0:T(8,128)} async-done(((f32[1024,1024]{1,0:T(8,128)}), f32[1024,128]{1,0:T(8,128)}) %reduce-scatter.5.cloned.1.call-update) | async-done | bytes 524304 | tf_op jit(solution)/shard_map/reduce_scatter | solution.py:91
  216.2 91.9 %reduce-scatter.3.cloned.1.call-done = f32[128,1024]{1,0:T(8,128)} async-done(((f32[1024,1024]{1,0:T(8,128)}), f32[128,1024]{1,0:T(8,128)}) %reduce-scatter.3.cloned.1.call-update) | async-done | bytes 524304 | tf_op jit(solution)/shard_map/reduce_scatter | solution.py:90
  (21 shorter events, 0.1 us)
Async XLA Ops:
  7.2 9.3 %copy-start = (bf16[1024,1024]{1,0:T(8,128)(2,1)S(1)}, bf16[1024,1024]{1,0:T(8,128)(2,1)}, u32[]{:S(2)}) copy-start(bf16[1024,1024]{1,0:T(8,128)(2,1)} %param.15) | copy-start | bytes 6291460
  7.2 3.1 copy-start.3
  7.2 3.1 copy-start.2
  7.2 3.5 %copy-start.4 = (bf16[1024]{0:T(1024)(128)(2,1)S(1)}, bf16[1024]{0:T(1024)(128)(2,1)}, u32[]{:S(2)}) copy-start(bf16[1024]{0:T(1024)(128)(2,1)} %param.13) | copy-start | bytes 6148
  7.2 48.5 %all-reduce.4.cloned.1.call-start = ((), (), s32[]{:S(2)}) async-start(), calls=%async_computation.6 | async-start | bytes 8388608 | tf_op jit(solution)/shard_map/psum | solution.py:83
  13.4 5.8 %copy-start.6 = (bf16[3072,1024]{1,0:T(8,128)(2,1)S(1)}, bf16[3072,1024]{1,0:T(8,128)(2,1)}, u32[]{:S(2)}) copy-start(bf16[3072,1024]{1,0:T(8,128)(2,1)} %param.10) | copy-start | bytes 18874372
  16.4 2.8 copy-start.7
  16.4 3.2 %copy-start.1 = (bf16[512,3072]{1,0:T(8,128)(2,1)S(1)}, bf16[512,3072]{1,0:T(8,128)(2,1)}, u32[]{:S(2)}) copy-start(bf16[512,3072]{1,0:T(8,128)(2,1)} %param.8) | copy-start | bytes 9437188
  24.4 0.7 copy-start.5
  29.6 31.2 %all-to-all-start = ((s32[8,1,128]{2,1,0:T(1,128)}), s32[8,1,128]{2,1,0:T(1,128)S(1)}, u32[]{:S(2)}, u32[]{:S(2)}) async-start(s32[8,1,128]{2,1,0:T(1,128)} %bitcast.3), calls=%async_computation | async-start | bytes 8192 | tf_op jit(solution)/shard_map/all_to_all | solution.py:39
  60.8 54.6 %all-to-all-start.1 = ((bf16[8,128,1024]{2,1,0:T(8,128)(2,1)}), bf16[8,128,1024]{2,1,0:T(8,128)(2,1)}, u32[]{:S(2)}, u32[]{:S(2)}) async-start(bf16[8,128,1024]{2,1,0:T(8,128)(2,1)} %bitcast.19), calls=%async_computation.1 | async-start | bytes 4194304 | tf_op jit(solution)/shard_map/all_to_all | solution.py:32
  66.6 149.6 %reduce-scatter.5.cloned.1.call-start = ((), (), s32[]{:S(2)}) async-start(), calls=%async_computation.5 | async-start | bytes 4718592 | tf_op jit(solution)/shard_map/reduce_scatter | solution.py:91
  128.5 179.5 %reduce-scatter.3.cloned.1.call-start = ((), (), s32[]{:S(2)}) async-start(), calls=%async_computation.4 | async-start | bytes 4718592 | tf_op jit(solution)/shard_map/reduce_scatter | solution.py:90
Sparse Core Ops, SparseCore 0:
  24.6 31.0 all-reduce.3
  128.7 87.4 reduce-scatter.4
  220.4 87.6 reduce-scatter.2
where the time goes:
time: 315 us
  waiting for transfers between devices  239 us (76%)
  matrix products  24.5 us (8%)
  between operations  13.9 us (4%)
  starting transfers between devices  13.2 us (4%)
  local copies, waits for them, and re-layouts  11.3 us (4%)
  other arithmetic  9.9 us (3%)
    reduce_scatter x1, waiting for transfers between devices, body(): lax.psum_scatter(local_up, 'batch', scatter_dimension=0, tiled=True)  91.9 us
    reduce_scatter x1, waiting for transfers between devices, body(): lax.psum_scatter(local_down, 'batch', scatter_dimension=1, tiled=True)  79.8 us
    all_to_all x1, waiting for transfers between devices, move_rows(): lax.all_to_all(buffer.reshape(peers, capacity, values.shape[1]), 'batch',...  48.6 us
    psum x1, waiting for transfers between devices, body(): out_full = lax.psum(out_part, 'tensor')  18.9 us
    dot_general x1, matrix products, body(): jnp.einsum('ti,th->ih', normed_s, dpre, preferred_element_type=jnp.float32)  7.82 us
    all_to_all x1, starting transfers between devices, move_rows(): lax.all_to_all(places.reshape(peers, capacity), 'batch', split_axis=0, co...  7.17 us
    scatter x1, local copies, waits for them, and re-layouts, move_rows(): return jnp.zeros_like(values).at[where.reshape(-1)].set(got.reshape(peers...  6.97 us
  transfers between devices with their start and end apart: 5, of which 4 were waited for; matrix products, arithmetic and copies ran while one was open for 6% of the time, Pallas kernels for 0%

commit v1 on v0

--- a/solution.py
+++ b/solution.py
@@ -1,9 +1,14 @@
+import functools
+
 import jax
 import jax.numpy as jnp
 from jax import lax
+from jax.experimental import pallas as pl
+from jax.experimental.pallas import tpu as pltpu
 from jax.sharding import PartitionSpec as P
 
 EPS = 1e-06
+MESH = pl.DeviceIdType.MESH
 
 
 def gelu_tanh(value):
@@ -45,6 +50,159 @@
         .at[where.reshape(-1)]
         .set(got.reshape(peers * capacity, values.shape[1]), mode="drop")
     )
+
+
+def grads_kernel(
+    length, norm_ref, dpre_ref, diff_ref, act_ref, up_ref, down_ref,
+    left_t, y_out, y_in, z_out, z_in, y_send, y_recv, z_send, z_recv,
+):
+    me = lax.axis_index("batch")
+    pos, side = me // 2, me % 2
+    other = 1 - side
+    half = pos // (length // 2)
+    block = up_ref.shape[0]
+    rights = (dpre_ref, act_ref)
+
+    barrier = pltpu.get_barrier_semaphore()
+    pl.semaphore_signal(barrier, inc=1, device_id={"batch": pos * 2 + other}, device_id_type=MESH)
+
+    @pl.when(pos > 0)
+    def _():
+        pl.semaphore_signal(barrier, inc=1, device_id={"batch": me - 2}, device_id_type=MESH)
+
+    @pl.when(pos < length - 1)
+    def _():
+        pl.semaphore_signal(barrier, inc=1, device_id={"batch": me + 2}, device_id_type=MESH)
+
+    left_t[0] = norm_ref[...].T
+    left_t[1] = diff_ref[...].T
+
+    pl.semaphore_wait(barrier, 1 + (pos + length - 1) // length + 1 - (pos + 1) // length)
+
+    def product(which, spot, at_side):
+        start = pl.multiple_of((spot * 2 + at_side) * block, block)
+        return jnp.dot(
+            left_t[which, pl.ds(start, block), :], rights[which][...],
+            preferred_element_type=jnp.float32,
+        )
+
+    def pair_copy(spot, which):
+        return pltpu.make_async_remote_copy(
+            src_ref=y_out.at[spot, which], dst_ref=y_in.at[spot, which],
+            send_sem=y_send.at[spot, which], recv_sem=y_recv.at[spot, which],
+            device_id={"batch": pos * 2 + other}, device_id_type=MESH,
+        )
+
+    def line_copy(way, step, which, target):
+        return pltpu.make_async_remote_copy(
+            src_ref=z_out.at[way, step, which], dst_ref=z_in.at[way, step, which],
+            send_sem=z_send.at[way, step, which], recv_sem=z_recv.at[way, step, which],
+            device_id={"batch": target}, device_id_type=MESH,
+        )
+
+    def moves():
+        for step in range(length - 1):
+            up_spot, down_spot = length - 1 - step, step
+            yield step, half, (1 - half) * up_spot + half * down_spot, 1 - 2 * half
+            yield step, 1 - half, half * up_spot + (1 - half) * down_spot, 2 * half - 1
+
+    def start_pair(spot):
+        for which in (1, 0):
+            y_out[spot, which] = product(which, spot, other).astype(y_out.dtype)
+            pair_copy(spot, which).start()
+
+    for step, way, spot, sign in moves():
+        @pl.when((spot - pos) * sign > 0)
+        def _():
+            start_pair(spot)
+
+    start_pair(pos)
+
+    for step, way, spot, sign in moves():
+        has_before = jnp.logical_and(pos - sign >= 0, pos - sign <= length - 1)
+
+        @pl.when((spot - pos) * sign > 0)
+        def _():
+            for which in (1, 0):
+                mine = product(which, spot, side)
+                pair_copy(spot, which).wait_recv()
+                mine = mine + y_in[spot, which].astype(jnp.float32)
+
+                @pl.when(has_before)
+                def _():
+                    line_copy(way, step, which, me).wait_recv()
+                    total = mine + z_in[way, step, which].astype(jnp.float32)
+                    z_out[way, step, which] = total.astype(z_out.dtype)
+
+                @pl.when(jnp.logical_not(has_before))
+                def _():
+                    z_out[way, step, which] = mine.astype(z_out.dtype)
+
+                line_copy(way, step, which, me + 2 * sign).start()
+
+    outs = (up_ref, down_ref)
+    for which in (1, 0):
+        mine = product(which, pos, side)
+        pair_copy(pos, which).wait_recv()
+        outs[which][...] = mine + y_in[pos, which].astype(jnp.float32)
+
+    for which in (1, 0):
+        @pl.when(pos > 0)
+        def _():
+            step = length - 1 - pos
+            line_copy(0, step, which, me).wait_recv()
+            outs[which][...] += z_in[0, step, which].astype(jnp.float32)
+
+        @pl.when(pos < length - 1)
+        def _():
+            line_copy(1, pos, which, me).wait_recv()
+            outs[which][...] += z_in[1, pos, which].astype(jnp.float32)
+
+    for spot in range(length):
+        for which in (1, 0):
+            pair_copy(spot, which).wait_send()
+    for step, way, spot, sign in moves():
+        @pl.when((spot - pos) * sign > 0)
+        def _():
+            for which in (1, 0):
+                line_copy(way, step, which, me).wait_send()
+
+
+def sum_grads(normed, dpre, diff, act):
+    peers = lax.axis_size("batch")
+    length = peers // 2
+    rows, inner = normed.shape
+    hidden = dpre.shape[1]
+    block = inner // peers
+    line_type = jnp.bfloat16 if length <= 4 else jnp.float32
+    vmem = pl.BlockSpec(memory_space=pltpu.VMEM)
+    result = jax.ShapeDtypeStruct((block, hidden), jnp.float32)
+    line = (2, length - 1, 2)
+    up, down_t = pl.pallas_call(
+        functools.partial(grads_kernel, length),
+        out_shape=(result, result),
+        in_specs=[vmem] * 4,
+        out_specs=(vmem, vmem),
+        scratch_shapes=[
+            pltpu.VMEM((2, inner, rows), jnp.bfloat16),
+            pltpu.VMEM((length, 2, block, hidden), jnp.bfloat16),
+            pltpu.VMEM((length, 2, block, hidden), jnp.bfloat16),
+            pltpu.VMEM(line + (block, hidden), line_type),
+            pltpu.VMEM(line + (block, hidden), line_type),
+            pltpu.SemaphoreType.DMA((length, 2)),
+            pltpu.SemaphoreType.DMA((length, 2)),
+            pltpu.SemaphoreType.DMA(line),
+            pltpu.SemaphoreType.DMA(line),
+        ],
+        compiler_params=pltpu.CompilerParams(
+            collective_id=1, has_side_effects=True, vmem_limit_bytes=56 * 1024 * 1024
+        ),
+        cost_estimate=pl.CostEstimate(
+            flops=4 * rows * inner * hidden, bytes_accessed=8 * rows * inner, transcendentals=0
+        ),
+        name="sum_grads",
+    )(normed, dpre, diff, act)
+    return up, down_t.T
 
 
 def body(
@@ -84,13 +242,7 @@
     diff = ((out_full - arrived.astype(jnp.float32)) * scale).astype(jnp.bfloat16)
     back = jnp.einsum("td,hd->th", diff, down_weight, preferred_element_type=jnp.float32)
     dpre = pull(back)[0].astype(jnp.bfloat16)
-    local_up = jnp.einsum("ti,th->ih", normed_s, dpre, preferred_element_type=jnp.float32)
-    local_down = jnp.einsum("th,td->hd", act, diff, preferred_element_type=jnp.float32)
-    grad_up, grad_down = (
-        lax.psum_scatter(local_up, "batch", scatter_dimension=0, tiled=True),
-        lax.psum_scatter(local_down, "batch", scatter_dimension=1, tiled=True),
-    )
-    return (grad_up, grad_down)
+    return sum_grads(normed_s, dpre, diff, act)
 
 
 def solution(mesh):

time: 315 us -> 197 us (0.63)
  waiting for transfers between devices: 239 us -> 67.7 us
  Pallas kernels: 0 us -> 51.4 us
  matrix products: 24.5 us -> 17.5 us
  other arithmetic: 9.9 us -> 15.1 us
  local copies, waits for them, and re-layouts: 11.3 us -> 14.7 us
    reduce_scatter x2 -> x0, waiting for transfers between devices: 172 us -> none  [the longest x1 91.9 us: body(): lax.psum_scatter(local_up, 'batch', scatter_dimension=0, tiled=True)]
    pallas_call x0 -> x1, Pallas kernels: none -> 51.4 us  [sum_grads(): pl.pallas_call(functools.partial(grads_kernel, length), out_shape=(result...]
    dot_general x2 -> x1, matrix products: 13.9 us -> 3.35 us  [body(): jnp.einsum('td,hd->th', diff, down_weight, preferred_element_type=jnp.flo...]
    unnamed x16 -> x20, local copies, waits for them, and re-layouts: 1.12 us -> 5.33 us
    dot_general x1, matrix products: 4.79 us -> 8.6 us  [body(): jnp.dot(normed_t, head_weight, preferred_element_type=jnp.float32)]
  transfers between devices with their start and end apart: 5 -> 3, of which waited for: 4 -> 2; matrix products, arithmetic and copies ran while one was open for 6% -> 5% of each run, Pallas kernels for 0% -> 0%
where the time goes in v1:
time: 197 us; the launch traced here: 196 us
  waiting for transfers between devices  67.7 us (34%)
  Pallas kernels  51.4 us (26%)
  matrix products  17.5 us (9%)
  other arithmetic  15.1 us (8%)
  local copies, waits for them, and re-layouts  14.7 us (7%)
  between operations  14.2 us (7%)
  starting transfers between devices  13 us (7%)
  blocking collectives  2.56 us (1%)
    pallas_call x1, Pallas kernels, sum_grads(): pl.pallas_call(functools.partial(grads_kernel, length), out_shape=(result...  51.4 us
    all_to_all x1, waiting for transfers between devices, move_rows(): lax.all_to_all(buffer.reshape(peers, capacity, values.shape[1]), 'batch',...  48.8 us
    psum x1, waiting for transfers between devices, body(): out_full = lax.psum(out_part, 'tensor')  18.9 us
    dot_general x1, matrix products, body(): jnp.dot(normed_t, head_weight, preferred_element_type=jnp.float32)  8.6 us
    all_to_all x1, starting transfers between devices, move_rows(): lax.all_to_all(places.reshape(peers, capacity), 'batch', split_axis=0, co...  7.16 us
    scatter x1, local copies, waits for them, and re-layouts, move_rows(): return jnp.zeros_like(values).at[where.reshape(-1)].set(got.reshape(peers...  6.15 us
    all_to_all x1, starting transfers between devices, move_rows(): lax.all_to_all(buffer.reshape(peers, capacity, values.shape[1]), 'batch',...  5.78 us
    unnamed x20, local copies, waits for them, and re-layouts  5.33 us
  transfers between devices with their start and end apart: 3, of which 2 were waited for; matrix products, arithmetic and copies ran while one was open for 5% of the time, Pallas kernels for 0%

profile of v1, /device:TPU:0, one launch (start us, length us, event | category | flops | bytes accessed | tf_op | source)
XLA Modules:
  0.0 196.1 jit_solution(12584302349758952576)
XLA Ops:
  7.2 0.0 copy-start
  7.2 0.0 all-reduce.4.cloned.1.call-start
  7.2 0.8 convert_element_type.41
  8.1 1.7 convert_reduce_fusion.1
  9.8 0.7 convert_element_type.47
  10.5 2.9 %convert_reduce_fusion = (f32[512]{0:T(512)S(1)}, f32[512]{0:T(512)S(1)}) fusion(bf16[512,3072]{1,0:T(8,128)(2,1)} %param.8), kind=kLoop, calls=%fused_computation.5 | loop fusion | flops 6290432 | bytes 3149824 | tf_op jit(solution)/shard_map/reduce_sum | solution.py:223
  13.4 0.4 fusion.18.norm_ref
  13.8 0.0 copy-start.5
  13.8 2.9 %multiply_convert_fusion.1 = (bf16[512,1024]{1,0:T(8,128)(2,1)S(1)}, f32[512,1024]{1,0:T(8,128)}) fusion(bf16[512,1024]{1,0:T(8,128)(2,1)S(1)} %fusion.18.norm_ref, bf16[1024,1024]{1,0:T(8,128)(2,1)S(1)} %copy-done), kind=kOutput, calls=%fused_computation.31 | convolution fusion | flops 1078460416 | bytes 6291456 | tf_op jit(solution)/shard_map/dot_general | solution.py:236
  16.7 2.6 %fusion.31 = f32[512,1024]{1,0:T(8,128)} fusion(bf16[512,1024]{1,0:T(8,128)(2,1)S(1)} %get-tuple-element.24.act_ref, bf16[1024,1024]{1,0:T(8,128)(2,1)S(1)} %copy-done.5), kind=kOutput, calls=%fused_computation.60 | convolution fusion | flops 1073741824 | bytes 5242880 | tf_op jit(solution)/shard_map/dot_general | solution.py:239
  19.3 2.6 %all-reduce = (f32[512]{0:T(512)S(1)}, f32[512]{0:T(512)S(1)}) all-reduce(f32[512]{0:T(512)S(1)} %get-tuple-element.11, f32[512]{0:T(512)S(1)} %get-tuple-element.10), channel_id=1, replica_groups=mesh['groups'=2,'batch'=8,'tensor'=2] {'tensor'}, use_global_device_ids=true, to_apply=%region_10.11 | all-reduce | flops 1024 | bytes 8192 | tf_op jit(solution)/shard_map/psum | solution.py:222
  21.9 8.6 %fusion.4 = f32[512,1024]{1,0:T(8,128)} fusion(bf16[3072,1024]{1,0:T(8,128)(2,1)} %param.10, bf16[512,3072]{1,0:T(8,128)(2,1)} %param.8, f32[3072]{0:T(1024)S(1)} %convert_element_type.47, f32[512]{0:T(512)S(1)} %get-tuple-element.21, f32[512]{0:T(512)S(1)} %get-tuple-element.20), kind=kOutput, calls=%fused_computation.10 | convolution fusion | flops 3229089792 | bytes 11550720 | tf_op jit(solution)/shard_map/dot_general | solution.py:228
  30.5 0.0 all-reduce.4.cloned.1.call-update
  30.5 0.7 copy-done.4
  31.2 1.1 reduce-window.6
  32.4 0.2 slice_reduce_fusion
  32.6 0.1 fusion.26
  32.7 3.0 %scatter_custom_fusion = s32[1024]{0:T(1024)} fusion(s32[512]{0:T(512)S(1)} %compare_select_fusion.1, s32[512]{0:T(512)S(1)} %get-tuple-element.18, s32[]{:T(128)} %constant.57.clone.1), kind=kCustom, calls=%fused_computation.53 | custom fusion | bytes 4100 | tf_op jit(solution)/shard_map/scatter | solution.py:35
  35.7 7.2 %all-to-all-start = ((s32[8,1,128]{2,1,0:T(1,128)}), s32[8,1,128]{2,1,0:T(1,128)S(1)}, u32[]{:S(2)}, u32[]{:S(2)}) async-start(s32[8,1,128]{2,1,0:T(1,128)} %bitcast.3), calls=%async_computation | async-start | bytes 8192 | tf_op jit(solution)/shard_map/all_to_all | solution.py:44
  42.9 18.9 %all-reduce.4.cloned.1.call-done = (f32[512,1024]{1,0:T(8,128)}, f32[512,1024]{1,0:T(8,128)}) async-done(((f32[512,1024]{1,0:T(8,128)}, f32[512,1024]{1,0:T(8,128)}), (f32[512,1024]{1,0:T(8,128)}, f32[512,1024]{1,0:T(8,128)})) %all-reduce.4.cloned.1.call-update) | async-done | bytes 4194320 | tf_op jit(solution)/shard_map/psum | solution.py:241
  61.8 5.2 %scatter_custom_fusion.1 = bf16[1024,1024]{1,0:T(8,128)(2,1)} fusion(s32[512]{0:T(512)S(1)} %compare_select_fusion.1, f32[512,1024]{1,0:T(8,128)} %get-tuple-element.17, bf16[]{:T(256)} %constant.56.clone.1), kind=kCustom, calls=%fused_computation.32 | custom fusion | flops 524288 | bytes 4194306 | tf_op jit(solution)/shard_map/scatter | solution.py:34
  67.0 5.8 %all-to-all-start.1 = ((bf16[8,128,1024]{2,1,0:T(8,128)(2,1)}), bf16[8,128,1024]{2,1,0:T(8,128)(2,1)}, u32[]{:S(2)}, u32[]{:S(2)}) async-start(bf16[8,128,1024]{2,1,0:T(8,128)(2,1)} %bitcast.23), calls=%async_computation.1 | async-start | bytes 4194304 | tf_op jit(solution)/shard_map/all_to_all | solution.py:37
  72.8 48.8 %all-to-all-done.1 = bf16[8,128,1024]{2,1,0:T(8,128)(2,1)} async-done(((bf16[8,128,1024]{2,1,0:T(8,128)(2,1)}), bf16[8,128,1024]{2,1,0:T(8,128)(2,1)}, u32[]{:S(2)}, u32[]{:S(2)}) %all-to-all-start.1) | async-done | bytes 2097184 | tf_op jit(solution)/shard_map/all_to_all | solution.py:37
  121.6 6.2 %scatter_custom_fusion.2 = bf16[512,1024]{1,0:T(8,128)(2,1)S(1)} fusion(s32[1024]{0:T(1024)S(1)} %bitcast.26, bf16[1024,1024]{1,0:T(8,128)(2,1)} %bitcast.7, bf16[]{:T(256)} %constant.56.clone.1), kind=kCustom, calls=%fused_computation.35 | custom fusion | bytes 1049088 | tf_op jit(solution)/shard_map/scatter | solution.py:51
  127.7 0.0 copy-start.6
  127.8 2.1 %multiply_convert_fusion.diff_ref = bf16[512,1024]{1,0:T(8,128)(2,1)S(1)} fusion(f32[512,1024]{1,0:T(8,128)} %get-tuple-element.16, bf16[512,1024]{1,0:T(8,128)(2,1)S(1)} %scatter_custom_fusion.2), kind=kLoop, calls=%fused_computation.30 | loop fusion | flops 2097152 | bytes 4194304 | tf_op jit(solution)/shard_map/convert_element_type | solution.py:242
  129.9 0.1 copy-done.6
  130.0 0.6 copy-done.8
  130.6 3.4 %fusion.15.dpre_ref = bf16[512,1024]{1,0:T(8,128)(2,1)} fusion(f32[512,1024]{1,0:T(8,128)S(1)} %copy-done.8, bf16[512,1024]{1,0:T(8,128)(2,1)S(1)} %multiply_convert_fusion.diff_ref, bf16[1024,1024]{1,0:T(8,128)(2,1)S(1)} %copy-done.6), kind=kOutput, calls=%fused_computation.25 | convolution fusion | flops 1084227584 | bytes 6291456 | tf_op jit(solution)/shard_map/td,hd->th/dot_general | solution.py:243
  133.9 51.4 %sum_grads.1 = (f32[128,1024]{1,0:T(8,128)}, f32[128,1024]{1,0:T(8,128)}) custom-call(bf16[512,1024]{1,0:T(8,128)(2,1)} %copy-done.2, bf16[512,1024]{1,0:T(8,128)(2,1)} %fusion.15.dpre_ref, bf16[512,1024]{1,0:T(8,128)(2,1)} %copy-done.3, bf16[512,1024]{1,0:T(8,128)(2,1)} %copy-done.7), custom_call_target="tpu_custom_call" | custom-call | flops 2147483648 | bytes 4194304 | tf_op jit(solution)/shard_map/sum_grads/pallas_call | solution.py:181
  185.3 2.0 %copy.11 = f32[1024,128]{1,0:T(8,128)} copy(f32[1024,128]{0,1:T(8,128)} %bitcast.24) | data formatting | bytes 1048576
  187.4 1.9 copy.15
  (21 shorter events, 0.1 us)
Async XLA Ops:
  7.2 6.6 %copy-start = (bf16[1024,1024]{1,0:T(8,128)(2,1)S(1)}, bf16[1024,1024]{1,0:T(8,128)(2,1)}, u32[]{:S(2)}) copy-start(bf16[1024,1024]{1,0:T(8,128)(2,1)} %param.14) | copy-start | bytes 6291460
  7.2 54.6 %all-reduce.4.cloned.1.call-start = ((), (), s32[]{:S(2)}) async-start(), calls=%async_computation.2 | async-start | bytes 8388608 | tf_op jit(solution)/shard_map/psum | solution.py:241
  8.0 5.3 %copy-start.1 = (bf16[512,1024]{1,0:T(8,128)(2,1)S(1)}, bf16[512,1024]{1,0:T(8,128)(2,1)}, u32[]{:S(2)}) copy-start(bf16[512,1024]{1,0:T(8,128)(2,1)} %param.12) | copy-start | bytes 3145732
  13.8 2.9 %copy-start.2 = (bf16[512,1024]{1,0:T(8,128)(2,1)}, bf16[512,1024]{1,0:T(8,128)(2,1)S(1)}, u32[]{:S(2)}) copy-start(bf16[512,1024]{1,0:T(8,128)(2,1)S(1)} %fusion.18.norm_ref) | copy-start | bytes 3145732
  13.8 2.9 %copy-start.5 = (bf16[1024,1024]{1,0:T(8,128)(2,1)S(1)}, bf16[1024,1024]{1,0:T(8,128)(2,1)}, u32[]{:S(2)}) copy-start(bf16[1024,1024]{1,0:T(8,128)(2,1)} %param.15) | copy-start | bytes 6291460
  16.7 2.6 %copy-start.7 = (bf16[512,1024]{1,0:T(8,128)(2,1)}, bf16[512,1024]{1,0:T(8,128)(2,1)S(1)}, u32[]{:S(2)}) copy-start(bf16[512,1024]{1,0:T(8,128)(2,1)S(1)} %get-tuple-element.24.act_ref) | copy-start | bytes 3145732
  30.5 0.7 copy-start.4
  35.7 31.2 %all-to-all-start = ((s32[8,1,128]{2,1,0:T(1,128)}), s32[8,1,128]{2,1,0:T(1,128)S(1)}, u32[]{:S(2)}, u32[]{:S(2)}) async-start(s32[8,1,128]{2,1,0:T(1,128)} %bitcast.3), calls=%async_computation | async-start | bytes 8192 | tf_op jit(solution)/shard_map/all_to_all | solution.py:44
  67.0 54.6 %all-to-all-start.1 = ((bf16[8,128,1024]{2,1,0:T(8,128)(2,1)}), bf16[8,128,1024]{2,1,0:T(8,128)(2,1)}, u32[]{:S(2)}, u32[]{:S(2)}) async-start(bf16[8,128,1024]{2,1,0:T(8,128)(2,1)} %bitcast.23), calls=%async_computation.1 | async-start | bytes 4194304 | tf_op jit(solution)/shard_map/all_to_all | solution.py:37
  127.7 2.2 %copy-start.6 = (bf16[1024,1024]{1,0:T(8,128)(2,1)S(1)}, bf16[1024,1024]{1,0:T(8,128)(2,1)}, u32[]{:S(2)}) copy-start(bf16[1024,1024]{1,0:T(8,128)(2,1)} %param.15) | copy-start | bytes 6291460
  127.7 2.8 %copy-start.8 = (f32[512,1024]{1,0:T(8,128)S(1)}, f32[512,1024]{1,0:T(8,128)}, u32[]{:S(2)}) copy-start(f32[512,1024]{1,0:T(8,128)} %get-tuple-element.25) | copy-start | bytes 6291460
  129.9 4.1 %copy-start.3 = (bf16[512,1024]{1,0:T(8,128)(2,1)}, bf16[512,1024]{1,0:T(8,128)(2,1)S(1)}, u32[]{:S(2)}) copy-start(bf16[512,1024]{1,0:T(8,128)(2,1)S(1)} %multiply_convert_fusion.diff_ref) | copy-start | bytes 3145732
Sparse Core Ops, SparseCore 0:
  30.7 31.0 all-reduce.3

commit v2 on v0

v2 whole, which is shorter than its diff:
```python
import functools

import jax
import jax.numpy as jnp
from jax import lax
from jax.experimental import pallas as pl
from jax.experimental.pallas import tpu as pltpu
from jax.sharding import PartitionSpec as P

EPS = 1e-06
MESH = pl.DeviceIdType.MESH


def step_kernel(
    length, cap, teacher_hbm, head_hbm, student_hbm, up_hbm, down_hbm, gain_t_ref, gain_s_ref,
    slot_row, slot_col, up_ref, down_ref,
    teacher, head, student, up, down, stat_out, stat_in, part, part_in, target,
    place_out, place_in, pack, got, flat_row, flat_col, norm, slope, act, out, out_in, arrived,
    diff, diff_in, dpre, left_t, y_out, y_in, z_out, z_in,
    load, core_send, core_recv, part_send, part_recv, place_send, place_recv, pack_send, pack_recv,
    y_send, y_recv, z_send, z_recv,
):
    me = lax.axis_index("batch")
    core = lax.axis_index("tensor")
    mate = 1 - core
    peers = 2 * length
    rows, wide = teacher.shape
    narrow = student.shape[1]
    cols = narrow // 2
    pos, side = me // 2, me % 2
    other = 1 - side
    half = pos // (length // 2)
    block = up_ref.shape[0]

    loads = [
        pltpu.make_async_copy(src, dst, load.at[i])
        for i, (src, dst) in enumerate(
            ((teacher_hbm, teacher), (head_hbm, head), (student_hbm, student), (up_hbm, up), (down_hbm, down))
        )
    ]
    for one in loads:
        one.start()

    barrier = pltpu.get_barrier_semaphore()
    pl.semaphore_signal(barrier, inc=1, device_id={"tensor": mate}, device_id_type=MESH)

    @pl.loop(1, peers)
    def _(i):
        pl.semaphore_signal(
            barrier, inc=1, device_id={"batch": (me + i) % peers}, device_id_type=MESH
        )

    def to_mate(index, src, dst):
        return pltpu.make_async_remote_copy(
            src_ref=src, dst_ref=dst, send_sem=core_send.at[index], recv_sem=core_recv.at[index],
            device_id={"tensor": mate}, device_id_type=MESH,
        )

    shift = rows.bit_length() - 1
    owner_row, owner_col = slot_row[...] >> shift, slot_col[...] >> shift
    same = owner_col == owner_row
    sub = lax.broadcasted_iota(jnp.int32, (rows, rows), 0)
    lane = lax.broadcasted_iota(jnp.int32, (rows, rows), 1)
    rank_row = jnp.sum(jnp.where(same & (sub < lane), 1, 0), axis=0, keepdims=True)
    rank_col = jnp.sum(jnp.where(same & (lane < sub), 1, 0), axis=1, keepdims=True)
    flat_row[...] = owner_row * cap + rank_row
    flat_col[...] = owner_col * cap + rank_col

    loads[0].wait()
    small = 32

    @pl.loop(0, rows // small)
    def _(i):
        at = pl.ds(pl.multiple_of(i * small, small), small)
        vals = teacher[at, :].astype(jnp.float32)
        total = jnp.sum(vals, axis=1, keepdims=True)
        squares = jnp.sum(vals * vals, axis=1, keepdims=True)
        spot = lax.broadcasted_iota(jnp.int32, (small, 128), 1)
        stat_out[at, :] = jnp.where(spot < 64, total, squares)

    pl.semaphore_wait(barrier, peers)
    swap_stat = to_mate(0, stat_out, stat_in)
    swap_stat.start()

    def place_copy(target_at, slot):
        return pltpu.make_async_remote_copy(
            src_ref=place_out.at[target_at], dst_ref=place_in.at[slot],
            send_sem=place_send.at[target_at], recv_sem=place_recv.at[slot],
            device_id={"batch": target_at}, device_id_type=MESH,
        )

    def places(target_at):
        spot = lax.broadcasted_iota(jnp.int32, (rows, cap), 1) + target_at * cap
        local = (slot_col[...] & (rows - 1)) + 1
        found = jnp.sum(jnp.where(flat_col[...] == spot, local, 0), axis=0, keepdims=True) - 1
        return jnp.broadcast_to(found, (8, cap))

    @pl.loop(1, peers)
    def _(i):
        target_at = (me + i) % peers
        place_out[target_at] = places(target_at)
        place_copy(target_at, me).start()

    place_in[me] = places(me)

    swap_stat.wait_recv()

    @pl.loop(0, rows // small)
    def _(i):
        at = pl.ds(pl.multiple_of(i * small, small), small)
        both = stat_out[at, :] + stat_in[at, :]
        mean = both[:, 0:1] / (2 * wide)
        var = both[:, 64:65] / (2 * wide) - mean * mean
        vals = teacher[at, :].astype(jnp.float32)
        scaled = (vals - mean) * lax.rsqrt(var + EPS) * gain_t_ref[...].astype(jnp.float32)
        teacher[at, :] = scaled.astype(jnp.bfloat16)

    loads[1].wait()
    large = rows // 2

    def part_copy(i):
        at = pl.ds(pl.multiple_of(i * large, large), large)
        return pltpu.make_async_remote_copy(
            src_ref=part.at[mate, at], dst_ref=part_in.at[at],
            send_sem=part_send.at[i], recv_sem=part_recv.at[i],
            device_id={"tensor": mate}, device_id_type=MESH,
        )

    @pl.loop(0, 2)
    def _(i):
        at = pl.ds(pl.multiple_of(i * large, large), large)
        value = jnp.dot(teacher[at, :], head[...], preferred_element_type=jnp.float32)
        part[0, at, :] = value[:, :cols]
        part[1, at, :] = value[:, cols:]
        part_copy(i).start()

    for i in range(2):
        part_copy(i).wait_recv()
        at = pl.ds(i * large, large)
        target[at, :] = (part[core, at, :] + part_in[at, :]).astype(jnp.bfloat16)

    def pack_copy(target_at, slot):
        return pltpu.make_async_remote_copy(
            src_ref=pack.at[target_at], dst_ref=got.at[slot],
            send_sem=pack_send.at[target_at], recv_sem=pack_recv.at[slot],
            device_id={"batch": target_at}, device_id_type=MESH,
        )

    def packed(target_at):
        spot = lax.broadcasted_iota(jnp.int32, (cap, rows), 0) + target_at * cap
        pick = jnp.where(flat_row[...] == spot, 1.0, 0.0).astype(jnp.bfloat16)
        return jnp.dot(pick, target[...], preferred_element_type=jnp.float32).astype(jnp.bfloat16)

    @pl.loop(1, peers)
    def _(i):
        target_at = (me + i) % peers
        pack[target_at] = packed(target_at)
        pack_copy(target_at, me).start()

    got[me] = packed(me)

    for one in loads[2:]:
        one.wait()
    middle = rows // 4
    root = 0.7978845608028654
    cube = 0.044715

    @pl.loop(0, rows // middle)
    def _(i):
        at = pl.ds(pl.multiple_of(i * middle, middle), middle)
        vals = student[at, :].astype(jnp.float32)
        mean = jnp.sum(vals, axis=1, keepdims=True) / narrow
        var = jnp.sum(vals * vals, axis=1, keepdims=True) / narrow - mean * mean
        scaled = (vals - mean) * lax.rsqrt(var + EPS) * gain_s_ref[...].astype(jnp.float32)
        norm[at, :] = scaled.astype(jnp.bfloat16)
        pre = jnp.dot(norm[at, :], up[...], preferred_element_type=jnp.float32)
        square = pre * pre
        bend = jnp.tanh(root * (pre + cube * (square * pre)))
        act[at, :] = (0.5 * pre * (1.0 + bend)).astype(jnp.bfloat16)
        slope[at, :] = 0.5 * (1.0 + bend) + 0.5 * pre * (1.0 - bend * bend) * (
            root * (1.0 + 3.0 * cube * square)
        )
        value = jnp.dot(act[at, :], down[...], preferred_element_type=jnp.float32)
        out[0, at, :] = value[:, :cols]
        out[1, at, :] = value[:, cols:]

    swap_out = to_mate(1, out.at[mate], out_in)
    swap_out.start()
    left_t[0] = norm[...].T
    swap_out.wait_recv()

    arrived[...] = jnp.zeros_like(arrived)

    def unpack(slot):
        spot = lax.broadcasted_iota(jnp.int32, (rows, cap), 0)
        put = jnp.where(place_in[slot, 0:1, :] == spot, 1.0, 0.0).astype(jnp.bfloat16)
        arrived[...] += jnp.dot(put, got[slot], preferred_element_type=jnp.float32)

    unpack(me)

    @pl.loop(1, peers)
    def _(i):
        source = (me + peers - i) % peers
        place_copy(source, source).wait_recv()
        pack_copy(source, source).wait_recv()
        unpack(source)

    scale = 1.0 / float(rows * peers) ** 0.5
    diff[...] = ((out[core] + out_in[...] - arrived[...]) * scale).astype(jnp.bfloat16)
    swap_diff = to_mate(2, diff, diff_in)
    swap_diff.start()
    left_t[1, pl.ds(pl.multiple_of(core * cols, cols), cols), :] = diff[...].T
    swap_diff.wait_recv()
    left_t[1, pl.ds(pl.multiple_of(mate * cols, cols), cols), :] = diff_in[...].T

    rights = (dpre, act)

    def product(which, spot, at_side):
        start = pl.multiple_of((spot * 2 + at_side) * block, block)
        return jnp.dot(
            left_t[which, pl.ds(start, block), :], rights[which][...],
            preferred_element_type=jnp.float32,
        )

    def pair_copy(spot, which):
        return pltpu.make_async_remote_copy(
            src_ref=y_out.at[spot, which], dst_ref=y_in.at[spot, which],
            send_sem=y_send.at[spot, which], recv_sem=y_recv.at[spot, which],
            device_id={"batch": pos * 2 + other}, device_id_type=MESH,
        )

    def line_copy(way, step, which, target_at):
        return pltpu.make_async_remote_copy(
            src_ref=z_out.at[way, step, which], dst_ref=z_in.at[way, step, which],
            send_sem=z_send.at[way, step, which], recv_sem=z_recv.at[way, step, which],
            device_id={"batch": target_at}, device_id_type=MESH,
        )

    def moves():
        for step in range(length - 1):
            up_spot, down_spot = length - 1 - step, step
            yield step, half, (1 - half) * up_spot + half * down_spot, 1 - 2 * half
            yield step, 1 - half, half * up_spot + (1 - half) * down_spot, 2 * half - 1

    def start_pairs(which):
        def start_pair(spot):
            y_out[spot, which] = product(which, spot, other).astype(y_out.dtype)
            pair_copy(spot, which).start()

        for step, way, spot, sign in moves():
            @pl.when((spot - pos) * sign > 0)
            def _():
                start_pair(spot)

        start_pair(pos)

    start_pairs(1)

    @pl.loop(0, rows // middle)
    def _(i):
        at = pl.ds(pl.multiple_of(i * middle, middle), middle)
        contract = (((1,), (1,)), ((), ()))

        def back_of(piece, which):
            lanes = pl.ds(pl.multiple_of(which * cols, cols), cols)
            return lax.dot_general(
                piece[at, :], down[:, lanes], contract, preferred_element_type=jnp.float32
            )

        back = back_of(diff, core) + back_of(diff_in, mate)
        dpre[at, :] = (back * slope[at, :]).astype(jnp.bfloat16)

    start_pairs(0)

    outs = (up_ref, down_ref)
    for which in (1, 0):
        for step, way, spot, sign in moves():
            has_before = jnp.logical_and(pos - sign >= 0, pos - sign <= length - 1)

            @pl.when((spot - pos) * sign > 0)
            def _():
                mine = product(which, spot, side)
                pair_copy(spot, which).wait_recv()
                mine = mine + y_in[spot, which].astype(jnp.float32)

                @pl.when(has_before)
                def _():
                    line_copy(way, step, which, me).wait_recv()
                    total = mine + z_in[way, step, which].astype(jnp.float32)
                    z_out[way, step, which] = total.astype(z_out.dtype)

                @pl.when(jnp.logical_not(has_before))
                def _():
                    z_out[way, step, which] = mine.astype(z_out.dtype)

                line_copy(way, step, which, me + 2 * sign).start()

    for which in (1, 0):
        mine = product(which, pos, side)
        pair_copy(pos, which).wait_recv()
        outs[which][...] = mine + y_in[pos, which].astype(jnp.float32)

    for which in (1, 0):
        @pl.when(pos > 0)
        def _():
            step = length - 1 - pos
            line_copy(0, step, which, me).wait_recv()
            outs[which][...] += z_in[0, step, which].astype(jnp.float32)

        @pl.when(pos < length - 1)
        def _():
            line_copy(1, pos, which, me).wait_recv()
            outs[which][...] += z_in[1, pos, which].astype(jnp.float32)

    swap_stat.wait_send()
    swap_out.wait_send()
    swap_diff.wait_send()
    for i in range(2):
        part_copy(i).wait_send()

    @pl.loop(1, peers)
    def _(i):
        target_at = (me + i) % peers
        place_copy(target_at, me).wait_send()
        pack_copy(target_at, me).wait_send()

    for which in (1, 0):
        for spot in range(length):
            pair_copy(spot, which).wait_send()
        for step, way, spot, sign in moves():
            @pl.when((spot - pos) * sign > 0)
            def _():
                line_copy(way, step, which, me).wait_send()


def body(
    teacher_rows,
    teacher_gain,
    head_weight,
    student_slot,
    student_rows,
    student_gain,
    up_weight,
    down_weight,
):
    peers = lax.axis_size("batch")
    length = peers // 2
    rows, wide = teacher_rows.shape
    narrow = student_rows.shape[1]
    hidden = up_weight.shape[1]
    cols = narrow // 2
    cap = 2 * rows // peers
    block = narrow // peers
    line_type = jnp.bfloat16 if length <= 4 else jnp.float32
    half, single = jnp.bfloat16, jnp.float32
    vmem = pl.BlockSpec(memory_space=pltpu.VMEM)
    far = pl.BlockSpec(memory_space=pl.ANY)
    result = jax.ShapeDtypeStruct((block, hidden), single)
    line = (2, length - 1, 2)
    dma = pltpu.SemaphoreType.DMA
    up, down_t = pl.pallas_call(
        functools.partial(step_kernel, length, cap),
        out_shape=(result, result),
        in_specs=[far] * 5 + [vmem] * 4,
        out_specs=(vmem, vmem),
        scratch_shapes=[
            pltpu.VMEM((rows, wide), half),
            pltpu.VMEM((wide, narrow), half),
            pltpu.VMEM((rows, narrow), half),
            pltpu.VMEM((narrow, hidden), half),
            pltpu.VMEM((hidden, narrow), half),
            pltpu.VMEM((rows, 128), single),
            pltpu.VMEM((rows, 128), single),
            pltpu.VMEM((2, rows, cols), single),
            pltpu.VMEM((rows, cols), single),
            pltpu.VMEM((rows, cols), half),
            pltpu.VMEM((peers, 8, cap), jnp.int32),
            pltpu.VMEM((peers, 8, cap), jnp.int32),
            pltpu.VMEM((peers, cap, cols), half),
            pltpu.VMEM((peers, cap, cols), half),
            pltpu.VMEM((1, rows), jnp.int32),
            pltpu.VMEM((rows, 1), jnp.int32),
            pltpu.VMEM((rows, narrow), half),
            pltpu.VMEM((rows, hidden), single),
            pltpu.VMEM((rows, hidden), half),
            pltpu.VMEM((2, rows, cols), single),
            pltpu.VMEM((rows, cols), single),
            pltpu.VMEM((rows, cols), single),
            pltpu.VMEM((rows, cols), half),
            pltpu.VMEM((rows, cols), half),
            pltpu.VMEM((rows, hidden), half),
            pltpu.VMEM((2, narrow, rows), half),
            pltpu.VMEM((length, 2, block, hidden), half),
            pltpu.VMEM((length, 2, block, hidden), half),
            pltpu.VMEM(line + (block, hidden), line_type),
            pltpu.VMEM(line + (block, hidden), line_type),
            dma((5,)),
            dma((3,)),
            dma((3,)),
            dma((2,)),
            dma((2,)),
            dma((peers,)),
            dma((peers,)),
            dma((peers,)),
            dma((peers,)),
            dma((length, 2)),
            dma((length, 2)),
            dma(line),
            dma(line),
        ],
        compiler_params=pltpu.CompilerParams(
            collective_id=1, has_side_effects=True, vmem_limit_bytes=60 * 1024 * 1024
        ),
        name="step",
    )(
        teacher_rows, head_weight, student_rows, up_weight, down_weight,
        teacher_gain.reshape(1, wide), student_gain.reshape(1, narrow),
        student_slot.reshape(1, rows), student_slot.reshape(rows, 1),
    )
    return up, down_t.T


def solution(mesh):
    return jax.shard_map(
        body,
        mesh=mesh,
        in_specs=(
            P(("groups", "batch"), "tensor"),
            P("tensor"),
            P("tensor", None),
            P(("groups", "batch")),
            P(("groups", "batch"), None),
            P(),
            P(None, "tensor"),
            P("tensor", None),
        ),
        out_specs=(P(("groups", "batch"), "tensor"), P(("groups", "tensor"), "batch")),
        check_vma=False,
    )
```

time: 315 us -> 108 us (0.34)
  waiting for transfers between devices: 239 us -> 0 us
  Pallas kernels: 0 us -> 98.6 us
  matrix products: 24.5 us -> 0 us
  between operations: 13.9 us -> 0.64 us
  starting transfers between devices: 13.2 us -> 0 us
  other arithmetic: 9.9 us -> 0 us
  local copies, waits for them, and re-layouts: 11.3 us -> 8.03 us
    reduce_scatter x2 -> x0, waiting for transfers between devices: 172 us -> none  [the longest x1 91.9 us: body(): lax.psum_scatter(local_up, 'batch', scatter_dimension=0, tiled=True)]
    pallas_call x0 -> x1, Pallas kernels: none -> 98.6 us  [body(): pl.pallas_call(functools.partial(step_kernel, length, cap), out_shape=(re...]
    all_to_all x2 -> x0, waiting for transfers between devices: 48.6 us -> none  [the longest x1 48.6 us: move_rows(): lax.all_to_all(buffer.reshape(peers, capacity, values.shape[1]), 'batch',...]
    dot_general x5 -> x0, matrix products: 24.5 us -> none  [the longest x1 7.82 us: body(): jnp.einsum('ti,th->ih', normed_s, dpre, preferred_element_type=jnp.float32)]
    psum x1 -> x0, waiting for transfers between devices: 18.9 us -> none  [body(): out_full = lax.psum(out_part, 'tensor')]
    all_to_all x2 -> x0, starting transfers between devices: 12.9 us -> none  [the longest x1 7.17 us: move_rows(): lax.all_to_all(places.reshape(peers, capacity), 'batch', split_axis=0, co...]
    scatter x2 -> x0, local copies, waits for them, and re-layouts: 9.98 us -> none  [the longest x1 6.97 us: move_rows(): return jnp.zeros_like(values).at[where.reshape(-1)].set(got.reshape(peers...]
    scatter x1 -> x0, other arithmetic: 5.13 us -> none  [move_rows(): jnp.zeros((peers * capacity, values.shape[1]), values.dtype).at[flat]]
  transfers between devices with their start and end apart: 5 -> 0, of which waited for: 4 -> 0; matrix products, arithmetic and copies ran while one was open for 6% -> 0% of each run, Pallas kernels for 0% -> 0%
where the time goes in v2:
time: 108 us; the launch traced here: 107 us
  Pallas kernels  98.6 us (91%)
  local copies, waits for them, and re-layouts  8.03 us (7%)
    pallas_call x1, Pallas kernels, body(): pl.pallas_call(functools.partial(step_kernel, length, cap), out_shape=(re...  98.6 us
    unnamed x2, local copies, waits for them, and re-layouts  3.92 us

profile of v2, /device:TPU:0, one launch (start us, length us, event | category | flops | bytes accessed | tf_op | source)
XLA Modules:
  0.0 107.3 jit_solution(3535596057864936372)
XLA Ops:
  0.6 1.3 %reshape.17.gain_s_ref = bf16[1,1024]{1,0:T(2,128)(2,1)} reshape(bf16[1024]{0:T(1024)(128)(2,1)} %param.13) | data formatting | bytes 4096 | tf_op jit(solution)/shard_map/reshape | solution.py:417
  1.9 1.3 %reshape.16.gain_t_ref = bf16[1,3072]{1,0:T(2,128)(2,1)} reshape(bf16[3072]{0:T(1024)(128)(2,1)} %param.9) | data formatting | bytes 12288 | tf_op jit(solution)/shard_map/reshape | solution.py:417
  3.2 1.5 %copy.11.slot_col = s32[512,1]{1,0:T(8,128)} copy(s32[512,1]{0,1:T(1,128)} %bitcast.4) | data formatting | bytes 4096 | tf_op jit(solution)/shard_map/reshape | solution.py:418
  4.7 98.6 %step.1 = (f32[128,1024]{1,0:T(8,128)}, f32[128,1024]{1,0:T(8,128)}) custom-call(bf16[512,3072]{1,0:T(8,128)(2,1)} %teacher_hbm.1, bf16[3072,1024]{1,0:T(8,128)(2,1)} %head_hbm.1, bf16[512,1024]{1,0:T(8,128)(2,1)} %student_hbm.1, bf16[1024,1024]{1,0:T(8,128)(2,1)} %up_hbm.1, bf16[1024,1024]{1,0:T(8,128)(2,1)} %down_hbm.1, ...), custom_call_target="tpu_custom_call" | custom-call | tf_op jit(solution)/shard_map/step/pallas_call | solution.py:361
  103.3 2.0 %copy.12 = f32[1024,128]{1,0:T(8,128)} copy(f32[1024,128]{0,1:T(8,128)} %bitcast.3) | data formatting | bytes 1048576
  105.4 1.9 %copy.14 = f32[128,1024]{1,0:T(8,128)} copy(f32[128,1024]{1,0:T(8,128)} %get-tuple-element.12) | data formatting | bytes 1048576

commit v3 on v2

--- a/solution.py
+++ b/solution.py
@@ -12,10 +12,10 @@
 
 
 def step_kernel(
-    length, cap, teacher_hbm, head_hbm, student_hbm, up_hbm, down_hbm, gain_t_ref, gain_s_ref,
-    slot_row, slot_col, up_ref, down_ref,
+    length, cap, teacher_hbm, head_hbm, student_hbm, up_hbm, down_hbm, gains_ref,
+    slot_row, up_ref, down_ref,
     teacher, head, student, up, down, stat_out, stat_in, part, part_in, target,
-    place_out, place_in, pack, got, flat_row, flat_col, norm, slope, act, out, out_in, arrived,
+    place_out, place_in, pack, got, slot_col, flat_row, flat_col, norm, slope, act, out, out_in, arrived,
     diff, diff_in, dpre, left_t, y_out, y_in, z_out, z_in,
     load, core_send, core_recv, part_send, part_recv, place_send, place_recv, pack_send, pack_recv,
     y_send, y_recv, z_send, z_recv,
@@ -27,6 +27,7 @@
     rows, wide = teacher.shape
     narrow = student.shape[1]
     cols = narrow // 2
+    chunk = cols // 2
     pos, side = me // 2, me % 2
     other = 1 - side
     half = pos // (length // 2)
@@ -57,6 +58,7 @@
         )
 
     shift = rows.bit_length() - 1
+    slot_col[...] = jnp.broadcast_to(slot_row[...], (128, rows)).T[:, 0:1]
     owner_row, owner_col = slot_row[...] >> shift, slot_col[...] >> shift
     same = owner_col == owner_row
     sub = lax.broadcasted_iota(jnp.int32, (rows, rows), 0)
@@ -112,52 +114,48 @@
         mean = both[:, 0:1] / (2 * wide)
         var = both[:, 64:65] / (2 * wide) - mean * mean
         vals = teacher[at, :].astype(jnp.float32)
-        scaled = (vals - mean) * lax.rsqrt(var + EPS) * gain_t_ref[...].astype(jnp.float32)
+        scaled = (vals - mean) * lax.rsqrt(var + EPS) * gains_ref[:, :wide]
         teacher[at, :] = scaled.astype(jnp.bfloat16)
 
     loads[1].wait()
-    large = rows // 2
-
-    def part_copy(i):
-        at = pl.ds(pl.multiple_of(i * large, large), large)
-        return pltpu.make_async_remote_copy(
-            src_ref=part.at[mate, at], dst_ref=part_in.at[at],
-            send_sem=part_send.at[i], recv_sem=part_recv.at[i],
+
+    def part_copy(c):
+        return pltpu.make_async_remote_copy(
+            src_ref=part.at[c], dst_ref=part_in.at[c],
+            send_sem=part_send.at[c], recv_sem=part_recv.at[c],
             device_id={"tensor": mate}, device_id_type=MESH,
         )
 
-    @pl.loop(0, 2)
-    def _(i):
-        at = pl.ds(pl.multiple_of(i * large, large), large)
-        value = jnp.dot(teacher[at, :], head[...], preferred_element_type=jnp.float32)
-        part[0, at, :] = value[:, :cols]
-        part[1, at, :] = value[:, cols:]
-        part_copy(i).start()
-
-    for i in range(2):
-        part_copy(i).wait_recv()
-        at = pl.ds(i * large, large)
-        target[at, :] = (part[core, at, :] + part_in[at, :]).astype(jnp.bfloat16)
-
-    def pack_copy(target_at, slot):
-        return pltpu.make_async_remote_copy(
-            src_ref=pack.at[target_at], dst_ref=got.at[slot],
-            send_sem=pack_send.at[target_at], recv_sem=pack_recv.at[slot],
+    def head_part(whose, c):
+        lanes = pl.ds(pl.multiple_of(whose * cols + c * chunk, chunk), chunk)
+        return jnp.dot(teacher[...], head[:, lanes], preferred_element_type=jnp.float32)
+
+    def pack_copy(c, target_at, slot):
+        return pltpu.make_async_remote_copy(
+            src_ref=pack.at[c, target_at], dst_ref=got.at[c, slot],
+            send_sem=pack_send.at[c, target_at], recv_sem=pack_recv.at[c, slot],
             device_id={"batch": target_at}, device_id_type=MESH,
         )
 
-    def packed(target_at):
+    def packed(c, target_at):
         spot = lax.broadcasted_iota(jnp.int32, (cap, rows), 0) + target_at * cap
         pick = jnp.where(flat_row[...] == spot, 1.0, 0.0).astype(jnp.bfloat16)
-        return jnp.dot(pick, target[...], preferred_element_type=jnp.float32).astype(jnp.bfloat16)
-
-    @pl.loop(1, peers)
-    def _(i):
-        target_at = (me + i) % peers
-        pack[target_at] = packed(target_at)
-        pack_copy(target_at, me).start()
-
-    got[me] = packed(me)
+        return jnp.dot(pick, target[c], preferred_element_type=jnp.float32).astype(jnp.bfloat16)
+
+    for c in range(2):
+        part[c] = head_part(mate, c)
+        part_copy(c).start()
+        mine = head_part(core, c)
+        part_copy(c).wait_recv()
+        target[c] = (mine + part_in[c]).astype(jnp.bfloat16)
+
+        @pl.loop(1, peers)
+        def _(i):
+            target_at = (me + i) % peers
+            pack[c, target_at] = packed(c, target_at)
+            pack_copy(c, target_at, me).start()
+
+        got[c, me] = packed(c, me)
 
     for one in loads[2:]:
         one.wait()
@@ -171,7 +169,7 @@
         vals = student[at, :].astype(jnp.float32)
         mean = jnp.sum(vals, axis=1, keepdims=True) / narrow
         var = jnp.sum(vals * vals, axis=1, keepdims=True) / narrow - mean * mean
-        scaled = (vals - mean) * lax.rsqrt(var + EPS) * gain_s_ref[...].astype(jnp.float32)
+        scaled = (vals - mean) * lax.rsqrt(var + EPS) * gains_ref[:, wide:]
         norm[at, :] = scaled.astype(jnp.bfloat16)
         pre = jnp.dot(norm[at, :], up[...], preferred_element_type=jnp.float32)
         square = pre * pre
@@ -189,29 +187,41 @@
     left_t[0] = norm[...].T
     swap_out.wait_recv()
 
-    arrived[...] = jnp.zeros_like(arrived)
-
-    def unpack(slot):
+    scale = 1.0 / float(rows * peers) ** 0.5
+
+    def put_of(slot):
         spot = lax.broadcasted_iota(jnp.int32, (rows, cap), 0)
-        put = jnp.where(place_in[slot, 0:1, :] == spot, 1.0, 0.0).astype(jnp.bfloat16)
-        arrived[...] += jnp.dot(put, got[slot], preferred_element_type=jnp.float32)
-
-    unpack(me)
-
-    @pl.loop(1, peers)
-    def _(i):
-        source = (me + peers - i) % peers
-        place_copy(source, source).wait_recv()
-        pack_copy(source, source).wait_recv()
-        unpack(source)
-
-    scale = 1.0 / float(rows * peers) ** 0.5
-    diff[...] = ((out[core] + out_in[...] - arrived[...]) * scale).astype(jnp.bfloat16)
-    swap_diff = to_mate(2, diff, diff_in)
-    swap_diff.start()
-    left_t[1, pl.ds(pl.multiple_of(core * cols, cols), cols), :] = diff[...].T
-    swap_diff.wait_recv()
-    left_t[1, pl.ds(pl.multiple_of(mate * cols, cols), cols), :] = diff_in[...].T
+        return jnp.where(place_in[slot, 0:1, :] == spot, 1.0, 0.0).astype(jnp.bfloat16)
+
+    def diff_copy(c):
+        return to_mate(2 + c, diff.at[c], diff_in.at[c])
+
+    def turn(c, whose, piece):
+        at = pl.ds(pl.multiple_of(whose * cols + c * chunk, chunk), chunk)
+        left_t[1, at, :] = piece[c].T
+
+    for c in range(2):
+        arrived[...] = jnp.dot(put_of(me), got[c, me], preferred_element_type=jnp.float32)
+
+        @pl.loop(1, peers)
+        def _(i):
+            source = (me + peers - i) % peers
+            if c == 0:
+                place_copy(source, source).wait_recv()
+            pack_copy(c, source, source).wait_recv()
+            arrived[...] += jnp.dot(
+                put_of(source), got[c, source], preferred_element_type=jnp.float32
+            )
+
+        lanes = slice(c * chunk, (c + 1) * chunk)
+        full = out[core, :, lanes] + out_in[:, lanes]
+        diff[c] = ((full - arrived[...]) * scale).astype(jnp.bfloat16)
+        diff_copy(c).start()
+        turn(c, core, diff)
+
+    for c in range(2):
+        diff_copy(c).wait_recv()
+        turn(c, mate, diff_in)
 
     rights = (dpre, act)
 
@@ -261,13 +271,14 @@
         at = pl.ds(pl.multiple_of(i * middle, middle), middle)
         contract = (((1,), (1,)), ((), ()))
 
-        def back_of(piece, which):
-            lanes = pl.ds(pl.multiple_of(which * cols, cols), cols)
+        def back_of(piece, whose, c):
+            lanes = pl.ds(pl.multiple_of(whose * cols + c * chunk, chunk), chunk)
             return lax.dot_general(
-                piece[at, :], down[:, lanes], contract, preferred_element_type=jnp.float32
+                piece[c, at, :], down[:, lanes], contract, preferred_element_type=jnp.float32
             )
 
-        back = back_of(diff, core) + back_of(diff_in, mate)
+        back = back_of(diff, core, 0) + back_of(diff, core, 1)
+        back = back + back_of(diff_in, mate, 0) + back_of(diff_in, mate, 1)
         dpre[at, :] = (back * slope[at, :]).astype(jnp.bfloat16)
 
     start_pairs(0)
@@ -314,15 +325,16 @@
 
     swap_stat.wait_send()
     swap_out.wait_send()
-    swap_diff.wait_send()
-    for i in range(2):
-        part_copy(i).wait_send()
+    for c in range(2):
+        part_copy(c).wait_send()
+        diff_copy(c).wait_send()
 
     @pl.loop(1, peers)
     def _(i):
         target_at = (me + i) % peers
         place_copy(target_at, me).wait_send()
-        pack_copy(target_at, me).wait_send()
+        for c in range(2):
+            pack_copy(c, target_at, me).wait_send()
 
     for which in (1, 0):
         for spot in range(length):
@@ -331,6 +343,11 @@
             @pl.when((spot - pos) * sign > 0)
             def _():
                 line_copy(way, step, which, me).wait_send()
+
+
+def place_kernel(up_ref, down_ref, up_out, down_out):
+    up_out[...] = up_ref[...]
+    down_out[...] = down_ref[...].T
 
 
 def body(
@@ -361,7 +378,7 @@
     up, down_t = pl.pallas_call(
         functools.partial(step_kernel, length, cap),
         out_shape=(result, result),
-        in_specs=[far] * 5 + [vmem] * 4,
+        in_specs=[far] * 5 + [vmem] * 2,
         out_specs=(vmem, vmem),
         scratch_shapes=[
             pltpu.VMEM((rows, wide), half),
@@ -371,13 +388,14 @@
             pltpu.VMEM((hidden, narrow), half),
             pltpu.VMEM((rows, 128), single),
             pltpu.VMEM((rows, 128), single),
-            pltpu.VMEM((2, rows, cols), single),
-            pltpu.VMEM((rows, cols), single),
-            pltpu.VMEM((rows, cols), half),
+            pltpu.VMEM((2, rows, cols // 2), single),
+            pltpu.VMEM((2, rows, cols // 2), single),
+            pltpu.VMEM((2, rows, cols // 2), half),
             pltpu.VMEM((peers, 8, cap), jnp.int32),
             pltpu.VMEM((peers, 8, cap), jnp.int32),
-            pltpu.VMEM((peers, cap, cols), half),
-            pltpu.VMEM((peers, cap, cols), half),
+            pltpu.VMEM((2, peers, cap, cols // 2), half),
+            pltpu.VMEM((2, peers, cap, cols // 2), half),
+            pltpu.VMEM((rows, 1), jnp.int32),
             pltpu.VMEM((1, rows), jnp.int32),
             pltpu.VMEM((rows, 1), jnp.int32),
             pltpu.VMEM((rows, narrow), half),
@@ -385,9 +403,9 @@
             pltpu.VMEM((rows, hidden), half),
             pltpu.VMEM((2, rows, cols), single),
             pltpu.VMEM((rows, cols), single),
-            pltpu.VMEM((rows, cols), single),
-            pltpu.VMEM((rows, cols), half),
-            pltpu.VMEM((rows, cols), half),
+            pltpu.VMEM((rows, cols // 2), single),
+            pltpu.VMEM((2, rows, cols // 2), half),
+            pltpu.VMEM((2, rows, cols // 2), half),
             pltpu.VMEM((rows, hidden), half),
             pltpu.VMEM((2, narrow, rows), half),
             pltpu.VMEM((length, 2, block, hidden), half),
@@ -395,14 +413,14 @@
             pltpu.VMEM(line + (block, hidden), line_type),
             pltpu.VMEM(line + (block, hidden), line_type),
             dma((5,)),
-            dma((3,)),
-            dma((3,)),
+            dma((4,)),
+            dma((4,)),
             dma((2,)),
             dma((2,)),
             dma((peers,)),
             dma((peers,)),
-            dma((peers,)),
-            dma((peers,)),
+            dma((2, peers)),
+            dma((2, peers)),
             dma((length, 2)),
             dma((length, 2)),
             dma(line),
@@ -414,10 +432,16 @@
         name="step",
     )(
         teacher_rows, head_weight, student_rows, up_weight, down_weight,
-        teacher_gain.reshape(1, wide), student_gain.reshape(1, narrow),
-        student_slot.reshape(1, rows), student_slot.reshape(rows, 1),
+        jnp.concatenate([teacher_gain, student_gain]).astype(single).reshape(1, wide + narrow),
+        student_slot.reshape(1, rows),
     )
-    return up, down_t.T
+    return pl.pallas_call(
+        place_kernel,
+        out_shape=(result, jax.ShapeDtypeStruct((hidden, block), single)),
+        in_specs=[vmem] * 2,
+        out_specs=(vmem, vmem),
+        name="place",
+    )(up, down_t)
 
 
 def solution(mesh):

time: 108 us -> 103 us (0.954)
  local copies, waits for them, and re-layouts: 8.03 us -> 1.39 us
  Pallas kernels: 98.6 us -> 99.9 us
    reshape x3 -> x0, local copies, waits for them, and re-layouts: 4.11 us -> none  [the longest x1 1.53 us: body(): student_slot.reshape(rows, 1)]
    unnamed x2 -> x0, local copies, waits for them, and re-layouts: 3.92 us -> none
    pallas_call x0 -> x1, Pallas kernels: none -> 2.31 us  [body(): pl.pallas_call(place_kernel, out_shape=(result, jax.ShapeDtypeStruct((hid...]
    concatenate x0 -> x2, local copies, waits for them, and re-layouts: none -> 1.39 us  [body(): jnp.concatenate([teacher_gain, student_gain]).astype(single)]
where the time goes in v3:
time: 103 us
  Pallas kernels  99.9 us (97%)
  local copies, waits for them, and re-layouts  1.39 us (1%)
    pallas_call x1, Pallas kernels, body(): pl.pallas_call(functools.partial(step_kernel, length, cap), out_shape=(re...  97.6 us
    pallas_call x1, Pallas kernels, body(): pl.pallas_call(place_kernel, out_shape=(result, jax.ShapeDtypeStruct((hid...  2.31 us

profile of v3, /device:TPU:0, one launch (start us, length us, event | category | flops | bytes accessed | tf_op | source)
XLA Modules:
  0.0 102.5 jit_solution(13020223993625634513)
XLA Ops:
  0.6 0.7 concatenate.15
  1.3 0.7 concatenate.14
  2.0 0.6 maximum_convert_fusion.gains_ref
  2.6 97.6 %step.1 = (f32[128,1024]{1,0:T(8,128)}, f32[128,1024]{1,0:T(8,128)}) custom-call(bf16[512,3072]{1,0:T(8,128)(2,1)} %teacher_hbm.1, bf16[3072,1024]{1,0:T(8,128)(2,1)} %head_hbm.1, bf16[512,1024]{1,0:T(8,128)(2,1)} %student_hbm.1, bf16[1024,1024]{1,0:T(8,128)(2,1)} %up_hbm.1, bf16[1024,1024]{1,0:T(8,128)(2,1)} %down_hbm.1, ...), custom_call_target="tpu_custom_call" | custom-call | tf_op jit(solution)/shard_map/step/pallas_call | solution.py:378
  100.2 2.3 %place.1 = (f32[128,1024]{1,0:T(8,128)}, f32[1024,128]{1,0:T(8,128)}) custom-call(f32[128,1024]{1,0:T(8,128)} %get-tuple-element.4.up_ref, f32[128,1024]{1,0:T(8,128)} %get-tuple-element.5.down_ref), custom_call_target="tpu_custom_call" | custom-call | tf_op jit(solution)/shard_map/place/pallas_call | solution.py:438

commit v4 on v3

--- a/solution.py
+++ b/solution.py
@@ -71,7 +71,7 @@
     loads[0].wait()
     small = 32
 
-    @pl.loop(0, rows // small)
+    @pl.loop(0, rows // small, unroll=4)
     def _(i):
         at = pl.ds(pl.multiple_of(i * small, small), small)
         vals = teacher[at, :].astype(jnp.float32)
@@ -107,7 +107,7 @@
 
     swap_stat.wait_recv()
 
-    @pl.loop(0, rows // small)
+    @pl.loop(0, rows // small, unroll=4)
     def _(i):
         at = pl.ds(pl.multiple_of(i * small, small), small)
         both = stat_out[at, :] + stat_in[at, :]

time: 103 us -> 101 us (0.981)
  Pallas kernels: 99.9 us -> 97.9 us
    pallas_call x1, Pallas kernels: 97.6 us -> 95.5 us  [body(): pl.pallas_call(functools.partial(step_kernel, length, cap), out_shape=(re...]
where the time goes in v4:
time: 101 us
  Pallas kernels  97.9 us (97%)
  local copies, waits for them, and re-layouts  1.39 us (1%)
    pallas_call x1, Pallas kernels, body(): pl.pallas_call(functools.partial(step_kernel, length, cap), out_shape=(re...  95.5 us
    pallas_call x1, Pallas kernels, body(): pl.pallas_call(place_kernel, out_shape=(result, jax.ShapeDtypeStruct((hid...  2.31 us

profile of v4, /device:TPU:0, one launch (start us, length us, event | category | flops | bytes accessed | tf_op | source)
XLA Modules:
  0.0 100.5 jit_solution(61548991926506354)
XLA Ops:
  0.6 0.7 concatenate.15
  1.3 0.7 concatenate.14
  2.0 0.6 maximum_convert_fusion.gains_ref
  2.6 95.5 %step.1 = (f32[128,1024]{1,0:T(8,128)}, f32[128,1024]{1,0:T(8,128)}) custom-call(bf16[512,3072]{1,0:T(8,128)(2,1)} %teacher_hbm.1, bf16[3072,1024]{1,0:T(8,128)(2,1)} %head_hbm.1, bf16[512,1024]{1,0:T(8,128)(2,1)} %student_hbm.1, bf16[1024,1024]{1,0:T(8,128)(2,1)} %up_hbm.1, bf16[1024,1024]{1,0:T(8,128)(2,1)} %down_hbm.1, ...), custom_call_target="tpu_custom_call" | custom-call | tf_op jit(solution)/shard_map/step/pallas_call | solution.py:378
  98.2 2.3 %place.1 = (f32[128,1024]{1,0:T(8,128)}, f32[1024,128]{1,0:T(8,128)}) custom-call(f32[128,1024]{1,0:T(8,128)} %get-tuple-element.4.up_ref, f32[128,1024]{1,0:T(8,128)} %get-tuple-element.5.down_ref), custom_call_target="tpu_custom_call" | custom-call | tf_op jit(solution)/shard_map/place/pallas_call | solution.py:438
